TPU v7x, 32 devices: a whole 2x2x4 slice. The times are simulated.
32 devices in a mesh: users: 4 (over y, x), items: 8 (over z, core).
Axes of the slice: x: 2, y: 2, z: 4, core: 2. Of those that a mesh axis runs over, the one named last changes fastest.
Arguments:
- user_emb: float32 [32768, 256], P(('users', 'items')), may hold values from -0.375 to 0.375
- item_emb: float32 [2048, 256], P('items'), may hold values from -0.375 to 0.375
- pos_blocks: int32 [32, 4], P(('users', 'items')), may hold values from 0 to 7, all different within a row
- neg_blocks: int32 [2], replicated, may hold values from 0 to 15
Outputs:
- user_new: float32 [32768, 256], P(('users', 'items'))
- item_new: float32 [2048, 256], P('items')
Inputs may be any that keep to these rules, and one draw needn't show every extreme that they name: `pos_blocks`: each row lists 4 different item blocks, and every item block is listed by some user block. `neg_blocks`: ids may repeat.
All inputs are finite; a program needn't handle non-finite values.
Results may differ from a plain program's by a relative error of at most 0.0003.
Values sent between devices are 32-bit elements; how exact they have to be, the bound alone decides.
A program may use at most 64 MiB of HBM per device.

v0:
```python
import jax
import jax.numpy as jnp
from jax import lax
from jax.sharding import PartitionSpec as P

NEGROWS = 128


SHARPNESS = 8.0
MARGIN = 2.0


def spread(array, axis, root):
    mine = lax.axis_index(axis) == root
    return lax.psum(jnp.where(mine, array, jnp.zeros_like(array)), axis)


def squares(rows):
    return jnp.sum(rows * rows, axis=-1)


def clipped(field):
    norms = jnp.sqrt(jnp.sum(field * field, axis=1, keepdims=True))
    return field / jnp.maximum(norms, 1.0)


def on_device(user_emb, item_emb, pos_blocks, neg_blocks):
    highest = lax.Precision.HIGHEST
    item_count = lax.axis_size("items")
    user_axis = lax.axis_size("users")
    own_index = lax.axis_index("items")
    user_count, embed_width = user_emb.shape
    block_rows = item_emb.shape[0]
    neg_count = neg_blocks.shape[0]
    pair_count = pos_blocks.shape[1]
    sub_count = block_rows // NEGROWS
    pieces = []
    for k in range(neg_count):
        owner_index = neg_blocks[k] // sub_count
        offset = neg_blocks[k] % sub_count * NEGROWS
        local_rows = lax.dynamic_slice_in_dim(item_emb, offset, NEGROWS, 0)
        pieces.append(spread(local_rows, "items", owner_index))
    negatives = jnp.concatenate(pieces, axis=0)
    products = jnp.dot(user_emb, negatives.T, precision=highest, preferred_element_type=jnp.float32)
    squared = squares(user_emb)[:, None] + squares(negatives)[None, :] - 2.0 * products
    weights = -jax.nn.sigmoid(SHARPNESS * (MARGIN - squared))
    user_grad = 2.0 * (
        jnp.sum(weights, axis=1)[:, None] * user_emb
        - jnp.dot(weights, negatives, precision=highest, preferred_element_type=jnp.float32)
    )
    neg_terms = 2.0 * (
        jnp.sum(weights, axis=0)[:, None] * negatives
        - jnp.dot(weights.T, user_emb, precision=highest, preferred_element_type=jnp.float32)
    )
    neg_total = lax.psum(neg_terms, ("users", "items"))
    gathered = lax.all_gather(item_emb, "items", axis=0, tiled=True).reshape(
        item_count, block_rows, embed_width
    )
    listed_ids = pos_blocks[0]
    listed = jnp.take(gathered, listed_ids, axis=0)
    products = jnp.einsum("re,kce->krc", user_emb, listed, precision=highest)
    squared = squares(user_emb)[None, :, None] + squares(listed)[:, None, :] - 2.0 * products
    weights = jax.nn.sigmoid(SHARPNESS * (squared - MARGIN))
    user_grad = user_grad + 2.0 * (
        jnp.sum(weights, axis=(0, 2))[:, None] * user_emb
        - jnp.einsum("krc,kce->re", weights, listed, precision=highest)
    )
    item_terms = 2.0 * (
        jnp.sum(weights, axis=1)[:, :, None] * listed
        - jnp.einsum("krc,re->kce", weights, user_emb, precision=highest)
    )
    buffer = (
        jnp.zeros((item_count, block_rows, embed_width), jnp.float32).at[listed_ids].add(item_terms)
    )
    item_grad = lax.psum_scatter(
        buffer.reshape(item_count * block_rows, embed_width),
        "items",
        scatter_dimension=0,
        tiled=True,
    )
    item_total = lax.psum(item_grad, "users")
    for k in range(neg_count):
        owner_index = neg_blocks[k] // sub_count
        offset = neg_blocks[k] % sub_count * NEGROWS
        contrib = jnp.where(
            owner_index == own_index, neg_total[k * NEGROWS : (k + 1) * NEGROWS], 0.0
        )
        current = lax.dynamic_slice_in_dim(item_total, offset, NEGROWS, 0)
        item_total = lax.dynamic_update_slice_in_dim(item_total, current + contrib, offset, 0)
    user_rate = 0.5 / (pair_count * block_rows + neg_count * NEGROWS)
    item_rate = 0.5 / (pair_count * user_count * user_axis)
    user_new = clipped(user_emb - user_rate * user_grad)
    item_new = clipped(item_emb - item_rate * item_total)
    return (user_new, item_new)


def solution(mesh):
    return jax.shard_map(
        on_device,
        mesh=mesh,
        in_specs=(P(("users", "items"), None), P("items", None), P(("users", "items"), None), P()),
        out_specs=(P(("users", "items"), None), P("items", None)),
        check_vma=False,
    )
```

profile of v0, /device:TPU:0, one launch (start us, length us, event | category | flops | bytes accessed | tf_op | source)
XLA Modules:
  0.0 323.8 jit_solution(6380355850158010825)
XLA Ops:
  7.2 0.0 copy-start.1
  7.2 0.0 all-gather.2.cloned.1.call-start
  7.2 0.7 all-gather.2.cloned.1.call-update
  7.9 0.0 all-reduce.9.cloned.1.call-start
  8.0 1.3 fusion.39
  14.5 1.7 dynamic-slice_select_fusion
  16.2 0.0 all-reduce.9.cloned.1.call-update
  16.2 0.0 reduce-scatter.2.cloned.1.call-start
  16.3 0.7 fusion.34
  16.9 0.7 compare_and_fusion
  17.6 1.5 multiply_reduce_fusion.2
  19.1 22.4 %all-gather.2.cloned.1.call-done = f32[2048,256]{1,0:T(8,128)} async-done(((f32[256,256]{1,0:T(8,128)}), f32[2048,256]{1,0:T(8,128)}) %all-gather.2.cloned.1.call-update) | async-done | bytes 2097168 | tf_op jit(solution)/shard_map/all_gather | solution.py:56
  41.4 2.2 gather_fusion
  43.7 0.3 multiply_reduce_fusion.1
  43.9 0.0 copy-done.1
  43.9 5.2 %fusion.37 = (f32[4,256]{1,0:T(4,128)S(1)}, f32[1024]{0:T(1024)S(1)}, f32[4,1024,256]{1,2,0:T(8,128)S(1)}) fusion(f32[1024,256]{1,0:T(8,128)S(1)} %copy-done.1, f32[4,256,256]{2,1,0:T(8,128)S(1)} %gather_fusion, pred[4]{0:T(512)(128)(4,1)S(1)} %compare_and_fusion, f32[4,256]{1,0:T(4,128)S(1)} %multiply_reduce_fusion.1, f32[1024]{0:T(1024)S(1)} %multiply_reduce_fusion.2), kind=kOutput, calls=%fused_computation.65 | convolution fusion | flops 3231971328 | bytes 6307844 | tf_op jit(solution)/shard_map/re,kce->krc/dot_general | solution.py:61
  49.1 1.9 copy-done
  51.0 3.4 %fusion.6 = f32[4,256,256]{2,1,0:T(8,128)S(1)} fusion(f32[4,1024,256]{1,2,0:T(8,128)S(1)} %get-tuple-element.14, f32[1024,256]{1,0:T(8,128)S(1)} %copy-done.1, f32[4,256,256]{2,1,0:T(8,128)S(1)} %gather_fusion, f32[4,256]{1,0:T(4,128)S(1)} %get-tuple-element.4, pred[4]{0:T(512)(128)(4,1)S(1)} %compare_and_fusion), kind=kOutput, calls=%fused_computation.10 | convolution fusion | flops 3222274048 | bytes 7344132 | tf_op jit(solution)/shard_map/krc,re->kce/dot_general | solution.py:70
  54.5 1.5 broadcast_in_dim.16
  56.0 3.1 scatter_fusion
  59.1 0.0 reduce-scatter.2.cloned.1.call-update
  59.2 0.2 all-reduce.7.cloned.1.call-start
  59.4 0.3 copy.10
  59.7 39.2 %all-reduce.9.cloned.1.call-done = (f32[128,256]{1,0:T(8,128)}, f32[128,256]{1,0:T(8,128)}) async-done(((f32[128,256]{1,0:T(8,128)}, f32[128,256]{1,0:T(8,128)}), (f32[128,256]{1,0:T(8,128)}, f32[128,256]{1,0:T(8,128)})) %all-reduce.9.cloned.1.call-update) | async-done | bytes 262160 | tf_op jit(solution)/shard_map/psum | solution.py:15
  99.0 0.9 constant_dynamic-update-slice_fusion.1
  99.9 0.9 constant_dynamic-update-slice_fusion
  100.8 0.0 copy-start.5
  100.8 0.1 multiply_reduce_fusion.4
  100.9 1.5 fusion.38
  102.4 0.0 copy-done.5
  102.4 0.9 copy-done.2
  103.4 1.8 fusion.19
  105.1 0.0 all-reduce.7.cloned.1.call-update
  105.2 0.0 all-reduce.5.cloned.1.call-start
  105.2 0.0 copy-start.6
  105.2 6.4 %fusion.18 = f32[1024,256]{0,1:T(8,128)S(1)} fusion(f32[4,1024,256]{1,2,0:T(8,128)} %copy-done, f32[1024,256]{0,1:T(8,128)S(1)} %copy.10, f32[4,256,256]{2,1,0:T(8,128)S(1)} %gather_fusion, f32[1024]{0:T(1024)S(1)} %get-tuple-element.5, pred[4]{0:T(512)(128)(4,1)S(1)} %compare_and_fusion), kind=kOutput, calls=%fused_computation.25 | convolution fusion | flops 3222011904 | bytes 7344132 | tf_op jit(solution)/shard_map/krc,kce->re/dot_general | solution.py:66
  111.6 0.0 copy-start.4
  111.6 1.4 multiply_reduce_fusion
  113.0 23.1 %reduce-scatter.2.cloned.1.call-done = f32[256,256]{1,0:T(8,128)} async-done(((f32[2048,256]{1,0:T(8,128)}), f32[256,256]{1,0:T(8,128)}) %reduce-scatter.2.cloned.1.call-update) | async-done | bytes 262160 | tf_op jit(solution)/shard_map/reduce_scatter | solution.py:75
  136.1 0.0 all-reduce.5.cloned.1.call-update
  136.2 0.1 broadcast_divide_fusion
  136.3 1.3 copy.11
  137.6 128.6 %all-reduce.7.cloned.1.call-done = f32[256,256]{1,0:T(8,128)} async-done(((f32[256,256]{1,0:T(8,128)}), f32[256,256]{1,0:T(8,128)}) %all-reduce.7.cloned.1.call-update) | async-done | bytes 262160 | tf_op jit(solution)/shard_map/psum | solution.py:55
  266.2 45.0 %all-reduce.5.cloned.1.call-done = f32[256,256]{1,0:T(8,128)} async-done(((f32[256,256]{1,0:T(8,128)}), f32[256,256]{1,0:T(8,128)}) %all-reduce.5.cloned.1.call-update) | async-done | bytes 262160 | tf_op jit(solution)/shard_map/psum | solution.py:81
  311.2 1.6 fusion.33
  312.8 1.6 fusion.31
  314.5 1.1 multiply_reduce_fusion.3
  315.5 1.8 broadcast_divide_fusion.1
  (11 shorter events, 0.0 us)
Async XLA Ops:
  7.2 36.8 %copy-start.1 = (f32[1024,256]{1,0:T(8,128)S(1)}, f32[1024,256]{1,0:T(8,128)}, u32[]{:S(2)}) copy-start(f32[1024,256]{1,0:T(8,128)} %param.4) | copy-start | bytes 3145732
  7.2 34.3 %all-gather.2.cloned.1.call-start = ((), (), s32[]{:S(2)}) async-start(), calls=%async_computation.1 | async-start | bytes 2359296 | tf_op jit(solution)/shard_map/all_gather | solution.py:56
  7.9 91.0 %all-reduce.9.cloned.1.call-start = ((), (), s32[]{:S(2)}) async-start(), calls=%async_computation.5 | async-start | bytes 524288 | tf_op jit(solution)/shard_map/psum | solution.py:15
  16.2 119.9 %reduce-scatter.2.cloned.1.call-start = ((), (), s32[]{:S(2)}) async-start(), calls=%async_computation.2 | async-start | bytes 2359296 | tf_op jit(solution)/shard_map/reduce_scatter | solution.py:75
  49.1 1.9 copy-start
  59.2 207.0 %all-reduce.7.cloned.1.call-start = ((), (), s32[]{:S(2)}) async-start(), calls=%async_computation.4 | async-start | bytes 524288 | tf_op jit(solution)/shard_map/psum | solution.py:55
  100.8 1.6 copy-start.5
  102.4 1.0 copy-start.2
  105.1 6.5 %copy-start.3 = (f32[1024,256]{0,1:T(8,128)S(1)}, f32[1024,256]{0,1:T(8,128)}, u32[]{:S(2)}) copy-start(f32[1024,256]{0,1:T(8,128)} %copy-done.2) | copy-start | bytes 3145732
  105.2 206.0 %all-reduce.5.cloned.1.call-start = ((), (), s32[]{:S(2)}) async-start(), calls=%async_computation.3 | async-start | bytes 524288 | tf_op jit(solution)/shard_map/psum | solution.py:81
  105.2 6.4 %copy-start.6 = (f32[256,256]{1,0:T(8,128)S(1)}, f32[256,256]{1,0:T(8,128)}, u32[]{:S(2)}) copy-start(f32[256,256]{1,0:T(8,128)} %copy-done.5) | copy-start | bytes 786436
  111.6 202.8 %copy-start.4 = (f32[256,256]{1,0:T(8,128)S(1)}, f32[256,256]{1,0:T(8,128)}, u32[]{:S(2)}) copy-start(f32[256,256]{1,0:T(8,128)} %param.5) | copy-start | bytes 786436
Sparse Core Ops, SparseCore 0:
  9.6 31.7 all-gather.1
  44.4 54.5 all-reduce.8
  101.4 34.7 reduce-scatter.1
  142.4 123.7 all-reduce.6
  269.2 41.9 all-reduce.4
where the time goes:
time: 324 us
  waiting for transfers between devices  259 us (80%)
  matrix products  19.6 us (6%)
  between operations  19.2 us (6%)
  other arithmetic  14.3 us (4%)
  local copies, waits for them, and re-layouts  11.4 us (4%)
    psum x1, waiting for transfers between devices, on_device(): neg_total = lax.psum(neg_terms, ('users', 'items'))  129 us
    psum x1, waiting for transfers between devices, on_device(): item_total = lax.psum(item_grad, 'users')  45 us
    psum x1, waiting for transfers between devices, spread(): return lax.psum(jnp.where(mine, array, jnp.zeros_like(array)), axis)  39.2 us
    reduce_scatter x1, waiting for transfers between devices, on_device(): lax.psum_scatter(buffer.reshape(item_count * block_rows, embed_width), 'i...  23.1 us
    all_gather x1, waiting for transfers between devices, on_device(): lax.all_gather(item_emb, 'items', axis=0, tiled=True)  22.4 us
  transfers between devices with their start and end apart: 5, of which 5 were waited for; matrix products, arithmetic and copies ran while one was open for 11% of the time, Pallas kernels for 0%

commit v1 on v0

v1 whole, which is shorter than its diff:
```python
import functools

import jax
import jax.numpy as jnp
from jax import lax
from jax.experimental import pallas as pl
from jax.experimental.pallas import tpu as pltpu
from jax.sharding import PartitionSpec as P

NEGROWS = 128
SHARPNESS = 8.0
MARGIN = 2.0
CHUNK = 512
MESH = pl.DeviceIdType.MESH


def split(x):
    high = x.astype(jnp.bfloat16)
    return high, (x - high.astype(jnp.float32)).astype(jnp.bfloat16)


def dot(a, b):
    return jnp.dot(a, b, preferred_element_type=jnp.float32)


def dot3(ah, al, bh, bl):
    return dot(ah, bh) + (dot(ah, bl) + dot(al, bh))


def clipped(field):
    norms = jnp.sqrt(jnp.sum(field * field, axis=1, keepdims=True))
    return field / jnp.maximum(norms, 1.0)


def kernel(
    n_users, n_items, user_rate, item_rate,
    user_ref, item_ref, pos_ref, neg_ref,
    user_out, item_out,
    mate, flags, uh, ul, uth, utl, ac, vbuf, vt, vth, vtl, vh, vl, bc,
    term, r1, psum, r2, gt, gu, rs, gsend, gmate,
    mate_s, mate_r, flag_s, flag_r, gm_s, gm_r,
    g1_s, g1_r, g2_s, g2_r, r1_s, r1_r, r2_s, r2_r, r3_s, r3_r,
):
    u = lax.axis_index("users")
    i = lax.axis_index("items")
    depth = n_items // 2
    z = i // 2
    c = i % 2
    other = 2 * z + (1 - c)
    rows, width = user_ref.shape
    cols = item_ref.shape[0]
    neg_count = neg_ref.shape[0]
    pair_count = pos_ref.shape[1]
    vrows = cols // n_users
    trows = width // n_users
    chunks = rows // CHUNK

    def plane(d):
        return ((u + d) % n_users, i)

    def up(s):
        return (u, 2 * ((z + s) % depth) + c)

    def down(s):
        return (u, 2 * ((z + depth - s) % depth) + c)

    def remote(src, dst, send, recv, where):
        return pltpu.make_async_remote_copy(
            src_ref=src, dst_ref=dst, send_sem=send, recv_sem=recv, device_id=where, device_id_type=MESH
        )

    barrier = pltpu.get_barrier_semaphore()
    pl.semaphore_signal(barrier, inc=1, device_id=(u, other), device_id_type=MESH)
    for d in range(1, n_users):
        pl.semaphore_signal(barrier, inc=1, device_id=plane(d), device_id_type=MESH)
    for s in range(1, depth):
        pl.semaphore_signal(barrier, inc=1, device_id=up(s), device_id_type=MESH)

    lane = lax.broadcasted_iota(jnp.int32, (8, 128), 1)
    listed = jnp.zeros((8, 128), jnp.float32)
    for k in range(pair_count):
        listed = listed + jnp.where(lane == pos_ref[0, k], 1.0, 0.0)
    flags[0] = listed

    pl.semaphore_wait(barrier, 1 + (n_users - 1) + (depth - 1))

    own_v = pl.ds(pl.multiple_of(u * vrows, vrows), vrows)
    own_t = pl.ds(pl.multiple_of(u * trows, trows), trows)

    g1 = {}
    for s in range(1, depth):
        g1[s] = remote(item_ref.at[own_v], vbuf.at[s, own_v], g1_s.at[s], g1_r.at[s], down(s))
        g1[s].start()
    mate_copy = remote(user_ref, mate, mate_s, mate_r, (u, other))
    mate_copy.start()
    flag_copy = remote(flags.at[0], flags.at[1], flag_s, flag_r, (u, other))
    flag_copy.start()

    def prepare_users(h, ref):
        @pl.loop(0, chunks)
        def _(k):
            at = pl.ds(pl.multiple_of(k * CHUNK, CHUNK), CHUNK)
            x = ref[at]
            ac[h, at] = 4.0 * jnp.sum(x * x, axis=1, keepdims=True) - 8.0
            high, low = split(-8.0 * x)
            uh[h, at] = high
            ul[h, at] = low
            high, low = split(x.T)
            uth[h, k] = high
            utl[h, k] = low
            gu[h, at] = jnp.zeros((CHUNK, width), jnp.float32)
            rs[h, at] = jnp.zeros((CHUNK, 128), jnp.float32)

    def prepare_items(s):
        x = item_ref[...] if s == 0 else vbuf[s]
        turned = x.T
        vt[s] = turned
        vth[s], vtl[s] = split(turned)
        vh[s], vl[s] = split(x)
        bc[s] = jnp.broadcast_to(4.0 * jnp.sum(turned * turned, axis=0, keepdims=True), (8, cols))
        term[s] = jnp.zeros((width, cols), jnp.float32)

    def unit(s, h):
        block = 2 * ((z + s) % depth) + c
        listed = jnp.sum(jnp.where(lane == block, flags[h], 0.0), axis=1, keepdims=True)[0:1]
        sub = block * (cols // NEGROWS) + lax.broadcasted_iota(jnp.int32, (1, cols), 1) // NEGROWS
        repeats = jnp.zeros((1, cols), jnp.float32)
        for k in range(neg_count):
            repeats = repeats + jnp.where(sub == neg_ref[k], 1.0, 0.0)
        slope = 0.5 * (listed + repeats)
        level = slope - repeats
        ahead = bc[s, 0:1]

        def step(k, total):
            at = pl.ds(pl.multiple_of(k * CHUNK, CHUNK), CHUNK)
            t = dot3(uh[h, at], ul[h, at], vth[s], vtl[s]) + (ac[h, at] + ahead)
            w = slope * jnp.tanh(t) + level
            wh, wl = split(w)
            gu[h, at] += dot3(wh, wl, vh[s], vl[s])
            part = w[:, 0:128]
            for b in range(1, cols // 128):
                part = part + w[:, b * 128 : (b + 1) * 128]
            rs[h, at] += part
            term[s] -= dot3(uth[h, k], utl[h, k], wh, wl)
            return total + jnp.sum(w, axis=0, keepdims=True)

        total = lax.fori_loop(0, chunks, step, jnp.zeros((1, cols), jnp.float32))
        term[s] += total * vt[s]

    g2 = {}

    def forward(s):
        g1[s].wait_recv()
        for d in range(1, n_users):
            g2[s, d] = remote(
                vbuf.at[s, own_v], vbuf.at[s, own_v], g2_s.at[s, d], g2_r.at[s, d], plane(d)
            )
            g2[s, d].start()

    r1c = {}
    r2c = {}

    def scatter(s):
        for d in range(1, n_users):
            to = (u + d) % n_users
            piece = pl.ds(pl.multiple_of(to * trows, trows), trows)
            r1c[s, d] = remote(
                term.at[s, piece], r1.at[d, s], r1_s.at[s, d], r1_r.at[s, d], plane(d)
            )
            r1c[s, d].start()

    def gather_sum(s):
        x = term[s, own_t]
        for d in range(1, n_users):
            r1c[s, d].wait_recv()
            x = x + r1[d, s]
        psum[s] = x
        if s:
            r2c[s] = remote(psum.at[s], r2.at[s], r2_s.at[s], r2_r.at[s], up(s))
            r2c[s].start()

    prepare_users(0, user_ref)
    prepare_items(0)
    forward(1)
    unit(0, 0)
    for s in range(2, depth):
        forward(s)
    mate_copy.wait_recv()
    flag_copy.wait_recv()
    prepare_users(1, mate)
    for s in range(1, depth):
        for d in range(1, n_users):
            g2[s, d].wait_recv()
        prepare_items(s)
        unit(s, 0)
        unit(s, 1)
        scatter(s)
        if s > 1:
            gather_sum(s - 1)
    unit(0, 1)
    scatter(0)
    gather_sum(depth - 1)

    def grad(h, ref, at):
        return jnp.sum(rs[h, at], axis=1, keepdims=True) * ref[at] - gu[h, at]

    @pl.loop(0, chunks)
    def _(k):
        at = pl.ds(pl.multiple_of(k * CHUNK, CHUNK), CHUNK)
        gsend[at] = grad(1, mate, at)

    gm_copy = remote(gsend, gmate, gm_s, gm_r, (u, other))
    gm_copy.start()

    gather_sum(0)
    x = psum[0]
    for s in range(1, depth):
        r2c[s].wait_recv()
        x = x + r2[s]
    gt[own_t] = x
    r3c = {}
    for d in range(1, n_users):
        r3c[d] = remote(gt.at[own_t], gt.at[own_t], r3_s.at[d], r3_r.at[d], plane(d))
        r3c[d].start()

    gm_copy.wait_recv()

    @pl.loop(0, chunks)
    def _(k):
        at = pl.ds(pl.multiple_of(k * CHUNK, CHUNK), CHUNK)
        total = grad(0, user_ref, at) + gmate[at]
        user_out[at] = clipped(user_ref[at] - (2.0 * user_rate) * total)

    for d in range(1, n_users):
        r3c[d].wait_recv()
    item_out[...] = clipped(item_ref[...] - (2.0 * item_rate) * gt[...].T)

    mate_copy.wait_send()
    flag_copy.wait_send()
    gm_copy.wait_send()
    for s in range(1, depth):
        g1[s].wait_send()
        r2c[s].wait_send()
        for d in range(1, n_users):
            g2[s, d].wait_send()
    for d in range(1, n_users):
        for s in range(depth):
            r1c[s, d].wait_send()
        r3c[d].wait_send()


def on_device(n_users, n_items, user_emb, item_emb, pos_blocks, neg_blocks):
    rows, width = user_emb.shape
    cols = item_emb.shape[0]
    neg_count = neg_blocks.shape[0]
    pair_count = pos_blocks.shape[1]
    depth = n_items // 2
    chunks = rows // CHUNK
    user_rate = 0.5 / (pair_count * cols + neg_count * NEGROWS)
    item_rate = 0.5 / (pair_count * rows * n_users)
    trows = width // n_users
    f32, b16 = jnp.float32, jnp.bfloat16
    dma = pltpu.SemaphoreType.DMA
    vmem = pl.BlockSpec(memory_space=pltpu.VMEM)
    smem = pl.BlockSpec(memory_space=pltpu.SMEM)
    scratch = [
        pltpu.VMEM((rows, width), f32),
        pltpu.VMEM((2, 8, 128), f32),
        pltpu.VMEM((2, rows, width), b16),
        pltpu.VMEM((2, rows, width), b16),
        pltpu.VMEM((2, chunks, width, CHUNK), b16),
        pltpu.VMEM((2, chunks, width, CHUNK), b16),
        pltpu.VMEM((2, rows, 1), f32),
        pltpu.VMEM((depth, cols, width), f32),
        pltpu.VMEM((depth, width, cols), f32),
        pltpu.VMEM((depth, width, cols), b16),
        pltpu.VMEM((depth, width, cols), b16),
        pltpu.VMEM((depth, cols, width), b16),
        pltpu.VMEM((depth, cols, width), b16),
        pltpu.VMEM((depth, 8, cols), f32),
        pltpu.VMEM((depth, width, cols), f32),
        pltpu.VMEM((n_users, depth, trows, cols), f32),
        pltpu.VMEM((depth, trows, cols), f32),
        pltpu.VMEM((depth, trows, cols), f32),
        pltpu.VMEM((width, cols), f32),
        pltpu.VMEM((2, rows, width), f32),
        pltpu.VMEM((2, rows, 128), f32),
        pltpu.VMEM((rows, width), f32),
        pltpu.VMEM((rows, width), f32),
        dma, dma, dma, dma, dma, dma,
        dma((depth,)), dma((depth,)),
        dma((depth, n_users)), dma((depth, n_users)),
        dma((depth, n_users)), dma((depth, n_users)),
        dma((depth,)), dma((depth,)),
        dma((n_users,)), dma((n_users,)),
    ]
    return pl.pallas_call(
        functools.partial(kernel, n_users, n_items, user_rate, item_rate),
        out_shape=(
            jax.ShapeDtypeStruct((rows, width), f32),
            jax.ShapeDtypeStruct((cols, width), f32),
        ),
        in_specs=[vmem, vmem, smem, smem],
        out_specs=(vmem, vmem),
        scratch_shapes=scratch,
        compiler_params=pltpu.CompilerParams(
            collective_id=0, has_side_effects=True, vmem_limit_bytes=48 * 1024 * 1024
        ),
        name="metric_step",
    )(user_emb, item_emb, pos_blocks, neg_blocks)


def solution(mesh):
    return jax.shard_map(
        functools.partial(on_device, mesh.shape["users"], mesh.shape["items"]),
        mesh=mesh,
        in_specs=(P(("users", "items"), None), P("items", None), P(("users", "items"), None), P()),
        out_specs=(P(("users", "items"), None), P("items", None)),
        check_vma=False,
    )
```

time: 324 us -> 47 us (0.15)
  waiting for transfers between devices: 259 us -> 0 us
  Pallas kernels: 0 us -> 41 us
  matrix products: 19.6 us -> 0 us
  between operations: 19.2 us -> 0.65 us
  other arithmetic: 14.3 us -> 0 us
  local copies, waits for them, and re-layouts: 11.4 us -> 5.15 us
    psum x3 -> x0, waiting for transfers between devices: 213 us -> none  [the longest x1 129 us: on_device(): neg_total = lax.psum(neg_terms, ('users', 'items'))]
    pallas_call x0 -> x1, Pallas kernels: none -> 41 us  [on_device(): pl.pallas_call(functools.partial(kernel, n_users, n_items, user_rate, ite...]
    reduce_scatter x1 -> x0, waiting for transfers between devices: 23.1 us -> none  [on_device(): lax.psum_scatter(buffer.reshape(item_count * block_rows, embed_width), 'i...]
    all_gather x1 -> x0, waiting for transfers between devices: 22.4 us -> none  [on_device(): lax.all_gather(item_emb, 'items', axis=0, tiled=True)]
    dot_general x6 -> x0, matrix products: 19.6 us -> none  [the longest x1 6.39 us: on_device(): jnp.einsum('krc,kce->re', weights, listed, precision=highest)]
    dynamic_update_slice x2 -> x0, other arithmetic: 3.27 us -> none  [on_device(): lax.dynamic_update_slice_in_dim(item_total, current + contrib, offset, 0)]
  transfers between devices with their start and end apart: 5 -> 0, of which waited for: 5 -> 0; matrix products, arithmetic and copies ran while one was open for 11% -> 0% of each run, Pallas kernels for 0% -> 0%
where the time goes in v1:
time: 47 us; the launch traced here: 46.8 us
  Pallas kernels  41 us (87%)
  local copies, waits for them, and re-layouts  5.15 us (11%)
  between operations  0.65 us (1%)
    pallas_call x1, Pallas kernels, on_device(): pl.pallas_call(functools.partial(kernel, n_users, n_items, user_rate, ite...  41 us
    unnamed x10, local copies, waits for them, and re-layouts  5.15 us

profile of v1, /device:TPU:0, one launch (start us, length us, event | category | flops | bytes accessed | tf_op | source)
XLA Modules:
  0.0 46.8 jit_solution(17328901549184936579)
XLA Ops:
  0.6 0.0 copy-start
  0.6 1.2 %copy-done = f32[1024,256]{1,0:T(8,128)S(1)} copy-done((f32[1024,256]{1,0:T(8,128)S(1)}, f32[1024,256]{1,0:T(8,128)}, u32[]{:S(2)}) %copy-start) | copy-done | bytes 1048600
  1.9 0.0 copy-start.1
  1.9 0.9 %copy-done.1 = f32[256,256]{1,0:T(8,128)S(1)} copy-done((f32[256,256]{1,0:T(8,128)S(1)}, f32[256,256]{1,0:T(8,128)}, u32[]{:S(2)}) %copy-start.1) | copy-done | bytes 262168
  2.8 0.0 copy-start.2
  2.8 0.7 %copy-done.2 = s32[1,4]{1,0:T(1,128)S(1)} copy-done((s32[1,4]{1,0:T(1,128)S(1)}, s32[1,4]{1,0:T(1,128)}, u32[]{:S(2)}) %copy-start.2) | copy-done | bytes 40
  3.5 0.0 copy-start.3
  3.5 0.7 %copy-done.3 = s32[2]{0:T(128)S(1)} copy-done((s32[2]{0:T(128)S(1)}, s32[2]{0:T(128)}, u32[]{:S(2)}) %copy-start.3) | copy-done | bytes 32
  4.1 41.0 %metric_step.1 = (f32[1024,256]{1,0:T(8,128)S(1)}, f32[256,256]{1,0:T(8,128)S(1)}) custom-call(f32[1024,256]{1,0:T(8,128)S(1)} %copy-done, f32[256,256]{1,0:T(8,128)S(1)} %copy-done.1, s32[1,4]{1,0:T(1,128)S(1)} %copy-done.2, s32[2]{0:T(128)S(1)} %copy-done.3), custom_call_target="tpu_custom_call" | custom-call | tf_op jit(solution)/shard_map/metric_step/pallas_call | solution.py:297
  45.1 1.0 %copy.8 = f32[1024,256]{1,0:T(8,128)} copy(f32[1024,256]{1,0:T(8,128)S(1)} %get-tuple-element.4) | data formatting | bytes 2097152
  46.1 0.7 %copy.9 = f32[256,256]{1,0:T(8,128)} copy(f32[256,256]{1,0:T(8,128)S(1)} %get-tuple-element.5) | data formatting | bytes 524288
Async XLA Ops:
  0.6 1.2 %copy-start = (f32[1024,256]{1,0:T(8,128)S(1)}, f32[1024,256]{1,0:T(8,128)}, u32[]{:S(2)}) copy-start(f32[1024,256]{1,0:T(8,128)} %user_ref.1) | copy-start | bytes 3145732
  1.9 0.9 %copy-start.1 = (f32[256,256]{1,0:T(8,128)S(1)}, f32[256,256]{1,0:T(8,128)}, u32[]{:S(2)}) copy-start(f32[256,256]{1,0:T(8,128)} %item_ref.1) | copy-start | bytes 786436
  2.8 0.7 %copy-start.2 = (s32[1,4]{1,0:T(1,128)S(1)}, s32[1,4]{1,0:T(1,128)}, u32[]{:S(2)}) copy-start(s32[1,4]{1,0:T(1,128)} %pos_ref.1) | copy-start | bytes 52
  3.5 0.7 %copy-start.3 = (s32[2]{0:T(128)S(1)}, s32[2]{0:T(128)}, u32[]{:S(2)}) copy-start(s32[2]{0:T(128)} %neg_ref.1) | copy-start | bytes 28

commit v2 on v1

--- a/solution.py
+++ b/solution.py
@@ -10,7 +10,7 @@
 NEGROWS = 128
 SHARPNESS = 8.0
 MARGIN = 2.0
-CHUNK = 512
+CHUNK = 1024
 MESH = pl.DeviceIdType.MESH
 
 
@@ -34,8 +34,9 @@
 
 def kernel(
     n_users, n_items, user_rate, item_rate,
-    user_ref, item_ref, pos_ref, neg_ref,
+    user_hbm, item_hbm, pos_hbm, neg_hbm,
     user_out, item_out,
+    user_ref, item_ref, pos_ref, neg_ref, load_s,
     mate, flags, uh, ul, uth, utl, ac, vbuf, vt, vth, vtl, vh, vl, bc,
     term, r1, psum, r2, gt, gu, rs, gsend, gmate,
     mate_s, mate_r, flag_s, flag_r, gm_s, gm_r,
@@ -55,6 +56,15 @@
     trows = width // n_users
     chunks = rows // CHUNK
 
+    loads = [
+        pltpu.make_async_copy(src, dst, load_s.at[n])
+        for n, (src, dst) in enumerate(
+            [(pos_hbm, pos_ref), (neg_hbm, neg_ref), (item_hbm, item_ref), (user_hbm, user_ref)]
+        )
+    ]
+    for load in loads:
+        load.start()
+
     def plane(d):
         return ((u + d) % n_users, i)
 
@@ -76,6 +86,8 @@
     for s in range(1, depth):
         pl.semaphore_signal(barrier, inc=1, device_id=up(s), device_id_type=MESH)
 
+    loads[0].wait()
+    loads[1].wait()
     lane = lax.broadcasted_iota(jnp.int32, (8, 128), 1)
     listed = jnp.zeros((8, 128), jnp.float32)
     for k in range(pair_count):
@@ -89,9 +101,9 @@
 
     g1 = {}
     for s in range(1, depth):
-        g1[s] = remote(item_ref.at[own_v], vbuf.at[s, own_v], g1_s.at[s], g1_r.at[s], down(s))
+        g1[s] = remote(item_hbm.at[own_v], vbuf.at[s, own_v], g1_s.at[s], g1_r.at[s], down(s))
         g1[s].start()
-    mate_copy = remote(user_ref, mate, mate_s, mate_r, (u, other))
+    mate_copy = remote(user_hbm, mate, mate_s, mate_r, (u, other))
     mate_copy.start()
     flag_copy = remote(flags.at[0], flags.at[1], flag_s, flag_r, (u, other))
     flag_copy.start()
@@ -179,7 +191,9 @@
             r2c[s] = remote(psum.at[s], r2.at[s], r2_s.at[s], r2_r.at[s], up(s))
             r2c[s].start()
 
+    loads[3].wait()
     prepare_users(0, user_ref)
+    loads[2].wait()
     prepare_items(0)
     forward(1)
     unit(0, 0)
@@ -199,8 +213,6 @@
             gather_sum(s - 1)
     unit(0, 1)
     scatter(0)
-    gather_sum(depth - 1)
-
     def grad(h, ref, at):
         return jnp.sum(rs[h, at], axis=1, keepdims=True) * ref[at] - gu[h, at]
 
@@ -211,8 +223,14 @@
 
     gm_copy = remote(gsend, gmate, gm_s, gm_r, (u, other))
     gm_copy.start()
-
+    gather_sum(depth - 1)
     gather_sum(0)
+
+    @pl.loop(0, chunks)
+    def _(k):
+        at = pl.ds(pl.multiple_of(k * CHUNK, CHUNK), CHUNK)
+        gu[0, at] = user_ref[at] - (2.0 * user_rate) * grad(0, user_ref, at)
+
     x = psum[0]
     for s in range(1, depth):
         r2c[s].wait_recv()
@@ -228,8 +246,7 @@
     @pl.loop(0, chunks)
     def _(k):
         at = pl.ds(pl.multiple_of(k * CHUNK, CHUNK), CHUNK)
-        total = grad(0, user_ref, at) + gmate[at]
-        user_out[at] = clipped(user_ref[at] - (2.0 * user_rate) * total)
+        user_out[at] = clipped(gu[0, at] - (2.0 * user_rate) * gmate[at])
 
     for d in range(1, n_users):
         r3c[d].wait_recv()
@@ -262,8 +279,13 @@
     f32, b16 = jnp.float32, jnp.bfloat16
     dma = pltpu.SemaphoreType.DMA
     vmem = pl.BlockSpec(memory_space=pltpu.VMEM)
-    smem = pl.BlockSpec(memory_space=pltpu.SMEM)
+    hbm = pl.BlockSpec(memory_space=pltpu.HBM)
     scratch = [
+        pltpu.VMEM((rows, width), f32),
+        pltpu.VMEM((cols, width), f32),
+        pltpu.SMEM(pos_blocks.shape, jnp.int32),
+        pltpu.SMEM(neg_blocks.shape, jnp.int32),
+        dma((4,)),
         pltpu.VMEM((rows, width), f32),
         pltpu.VMEM((2, 8, 128), f32),
         pltpu.VMEM((2, rows, width), b16),
@@ -300,11 +322,11 @@
             jax.ShapeDtypeStruct((rows, width), f32),
             jax.ShapeDtypeStruct((cols, width), f32),
         ),
-        in_specs=[vmem, vmem, smem, smem],
+        in_specs=[pl.BlockSpec(memory_space=pl.ANY)] * 4,
         out_specs=(vmem, vmem),
         scratch_shapes=scratch,
         compiler_params=pltpu.CompilerParams(
-            collective_id=0, has_side_effects=True, vmem_limit_bytes=48 * 1024 * 1024
+            collective_id=0, has_side_effects=True, vmem_limit_bytes=60 * 1024 * 1024
         ),
         name="metric_step",
     )(user_emb, item_emb, pos_blocks, neg_blocks)

time: 47 us -> 44.7 us (0.951)
  local copies, waits for them, and re-layouts: 5.15 us -> 3.01 us
    unnamed x10 -> x4, local copies, waits for them, and re-layouts: 5.15 us -> 3.01 us
where the time goes in v2:
time: 44.7 us; the launch traced here: 44.5 us
  Pallas kernels  40.9 us (91%)
  local copies, waits for them, and re-layouts  3.01 us (7%)
  between operations  0.65 us (1%)
    pallas_call x1, Pallas kernels, on_device(): pl.pallas_call(functools.partial(kernel, n_users, n_items, user_rate, ite...  40.9 us
    unnamed x4, local copies, waits for them, and re-layouts  3.01 us

profile of v2, /device:TPU:0, one launch (start us, length us, event | category | flops | bytes accessed | tf_op | source)
XLA Modules:
  0.0 44.5 jit_solution(7111095992217604599)
XLA Ops:
  0.6 40.9 %metric_step.1 = (f32[1024,256]{1,0:T(8,128)}, f32[256,256]{1,0:T(8,128)}) custom-call(f32[1024,256]{1,0:T(8,128)} %user_hbm.1, f32[256,256]{1,0:T(8,128)} %item_hbm.1, s32[1,4]{1,0:T(1,128)} %pos_hbm.1, s32[2]{0:T(128)} %neg_hbm.1), custom_call_target="tpu_custom_call" | custom-call | tf_op jit(solution)/shard_map/metric_step/pallas_call | solution.py:319
  41.5 0.0 copy-start
  41.5 2.3 %copy.8 = f32[1024,256]{1,0:T(8,128)} copy(f32[1024,256]{1,0:T(8,128)} %get-tuple-element.4) | data formatting | bytes 2097152
  43.8 0.0 copy-done
  43.8 0.7 %copy.9 = f32[256,256]{1,0:T(8,128)} copy(f32[256,256]{1,0:T(8,128)S(1)} %copy-done) | data formatting | bytes 524288
Async XLA Ops:
  41.5 2.3 %copy-start = (f32[256,256]{1,0:T(8,128)S(1)}, f32[256,256]{1,0:T(8,128)}, u32[]{:S(2)}) copy-start(f32[256,256]{1,0:T(8,128)} %get-tuple-element.5) | copy-start | bytes 786436
